TPU v7x, 128 devices: a whole 4x4x4 slice. The times are simulated.
128 devices in a mesh: aux: 4 (over x), pair: 32 (over z, y, core).
Axes of the slice: x: 4, y: 4, z: 4, core: 2. Of those that a mesh axis runs over, the one named last changes fastest.
Arguments:
- three_index: bfloat16 [512, 256, 2048], P('pair', None, 'aux'), may hold values from -0.875 to 0.875
- fock_diag: float32 [512], replicated, may hold values from -1.2 to -0.3
- pair_occ: int32 [992, 2], P('pair'), may hold values from 0 to 511, as said below
- pno_count: int32 [992], P('pair'), may hold values from 32 to 128
- pno_energy: float32 [992, 128], P('pair'), may hold values from 0.3 to 3
- pno_coef: bfloat16 [992, 2, 256, 128], P('pair'), may hold values from -0.375 to 0.375
Outputs:
- pair_energy: float32 [992], P('pair')
- grad_ints: float32 [512, 256, 2048], P('pair', None, 'aux')
Inputs may be any that keep to these rules, and one draw needn't show every extreme that they name: `pair_occ`: orbital o belongs to the block o // 16. Among the 62 orbitals named by the pairs of one aligned block of 31 rows, at most 2 belong to any one orbital block, and one orbital block receives exactly 2 from every such row block; i may equal j.
All inputs are finite; a program needn't handle non-finite values.
Results may differ from a plain program's by a relative error of at most 0.0061.
Values may be sent and summed in bfloat16 or wider, within the bound.
A program may use at most 128 MiB of HBM per device.

v0:
```python
import jax
import jax.numpy as jnp
from jax import lax
from jax.sharding import PartitionSpec as P


def local(three_index, fock_diag, pair_occ, pno_count, pno_energy, pno_coef):
    groups = lax.axis_size("pair")
    occ_dev = three_index.shape[0]
    width_dom = three_index.shape[1]
    width_aux = three_index.shape[2]
    pair_dev = pair_occ.shape[0]
    width_pno = pno_coef.shape[3]
    halves = 2 * pair_dev
    capacity = max(2, halves // groups + 1)
    slots = groups * capacity
    occ_flat = pair_occ.reshape(halves)
    owner_of = occ_flat // occ_dev
    local_index = occ_flat % occ_dev
    owner_hot = (owner_of[:, None] == jnp.arange(groups, dtype=jnp.int32)[None, :]).astype(
        jnp.int32
    )
    before = jnp.cumsum(owner_hot, axis=0) - owner_hot
    rank_in = jnp.sum(before * owner_hot, axis=1)
    slot_of = owner_of * capacity + rank_in
    request = jnp.zeros((slots,), jnp.int32).at[slot_of].set(local_index + 1)
    arrived = lax.all_to_all(
        request.reshape(groups, capacity), "pair", split_axis=0, concat_axis=0, tiled=True
    ).reshape(slots)
    is_live = arrived > 0
    row_index = jnp.maximum(arrived - 1, 0)
    selected = jnp.take(three_index, row_index, axis=0)
    selected = jnp.where(is_live[:, None, None], selected, jnp.zeros_like(selected))
    coef_half = pno_coef.reshape(halves, width_dom, width_pno)
    rows_back = lax.all_to_all(
        selected.reshape(groups, capacity, width_dom, width_aux),
        "pair",
        split_axis=0,
        concat_axis=0,
        tiled=True,
    )
    mine = jnp.take(rows_back.reshape(slots, width_dom, width_aux), slot_of, axis=0)
    projected = jnp.einsum(
        "hdp,hdq->hpq", coef_half, mine, preferred_element_type=jnp.float32
    ).astype(jnp.bfloat16)
    paired = projected.reshape(pair_dev, 2, width_pno, width_aux)
    rows_i = paired[:, 0]
    rows_j = paired[:, 1]
    partial_sum = jnp.einsum("kpq,krq->kpr", rows_i, rows_j, preferred_element_type=jnp.float32)
    coupling = lax.psum(partial_sum, "aux")
    fock_i = jnp.take(fock_diag, pair_occ[:, 0])
    fock_j = jnp.take(fock_diag, pair_occ[:, 1])
    denom = pno_energy[:, :, None] + pno_energy[:, None, :] - (fock_i + fock_j)[:, None, None]
    in_pno = jnp.arange(width_pno, dtype=jnp.int32)[None, :] < pno_count[:, None]
    both_in = in_pno[:, :, None] & in_pno[:, None, :]
    amplitude = jnp.where(both_in, -coupling / denom, jnp.float32(0.0))
    mixed = 2.0 * amplitude - jnp.swapaxes(amplitude, 1, 2)
    energy = jnp.sum(coupling * mixed, axis=(1, 2)) / (width_pno * width_pno)
    weights = mixed.astype(jnp.bfloat16)
    gamma_i = jnp.einsum(
        "kab,kbq->kaq", weights, rows_j, preferred_element_type=jnp.float32
    ).astype(jnp.bfloat16)
    gamma_j = jnp.einsum(
        "kba,kbq->kaq", weights, rows_i, preferred_element_type=jnp.float32
    ).astype(jnp.bfloat16)
    gamma = jnp.stack([gamma_i, gamma_j], axis=1).reshape(halves, width_pno, width_aux)
    dom_terms = jnp.einsum(
        "hdp,hpq->hdq", coef_half, gamma, preferred_element_type=jnp.float32
    ).astype(jnp.bfloat16)
    term_send = jnp.zeros((slots, width_dom, width_aux), jnp.bfloat16).at[slot_of].set(dom_terms)
    terms = lax.all_to_all(
        term_send.reshape(groups, capacity, width_dom, width_aux),
        "pair",
        split_axis=0,
        concat_axis=0,
        tiled=True,
    )
    terms = terms.reshape(slots, width_dom, width_aux)
    occ_hot = (row_index[None, :] == jnp.arange(occ_dev, dtype=jnp.int32)[:, None]) & is_live[
        None, :
    ]
    grad = jnp.dot(
        occ_hot.astype(jnp.bfloat16),
        terms.reshape(slots, width_dom * width_aux),
        preferred_element_type=jnp.float32,
    )
    return (energy, grad.reshape(occ_dev, width_dom, width_aux))


def solution(mesh):
    placed = (
        P("pair", None, "aux"),
        P(),
        P("pair", None),
        P("pair"),
        P("pair", None),
        P("pair", None, None, None),
    )
    return jax.shard_map(
        local,
        mesh=mesh,
        in_specs=placed,
        out_specs=(P("pair"), P("pair", None, "aux")),
        check_vma=False,
    )
```

profile of v0, /device:TPU:0, one launch (start us, length us, event | category | flops | bytes accessed | tf_op | source)
XLA Modules:
  0.0 715.7 jit_solution(3268946440946229828)
XLA Ops:
  7.2 0.0 copy-start
  7.2 0.8 copy.56
  8.0 0.1 reshape.245
  8.1 0.1 reshape.244
  8.2 0.1 fusion.14
  8.3 0.1 reduce_window_sum.11
  8.4 0.2 select_reduce_fusion
  8.6 0.8 scatter_custom_fusion
  9.3 0.1 all_to_all.12
  9.4 15.6 %all_to_all.19 = s32[32,1,2]{2,1,0:T(1,128)S(1)} all-to-all(s32[32,1,2]{2,1,0:T(1,128)S(1)} %bitcast.90), channel_id=1, replica_groups=mesh['aux'=4,'pair'=32] {'pair'}, dimensions={0} | all-to-all | bytes 512 | tf_op jit(solution)/shard_map/all_to_all | solution.py:27
  25.0 0.1 copy.59
  25.1 0.1 copy.62
  25.2 0.1 copy.60
  25.3 0.1 copy.63
  25.4 0.1 reshape.269
  25.5 9.8 %gather_fusion = bf16[64,256,512]{2,1,0:T(8,128)(2,1)} fusion(bf16[16,256,512]{2,1,0:T(8,128)(2,1)} %param.8, s32[1024]{0:T(1024)S(1)} %pad_clamp_fusion.3), kind=kCustom, calls=%fused_computation.2 | custom fusion | bytes 33554688 | tf_op jit(solution)/shard_map/jit(_take)/gather | solution.py:32
  35.3 14.3 %select_select_fusion = bf16[32,2,256,512]{3,2,1,0:T(8,128)(2,1)} fusion(bf16[32,2,256,512]{3,2,1,0:T(8,128)(2,1)} %bitcast.81, pred[32,2]{1,0:T(8,128)(4,1)S(1)} %copy.62, pred[32,2]{1,0:T(8,128)(4,1)S(1)} %copy.60), kind=kLoop, calls=%fused_computation.9 | loop fusion | flops 16777216 | bytes 33554560 | tf_op jit(solution)/shard_map/jit(_where)/select_n | solution.py:33
  49.6 5.2 all-to-all-start.1
  54.8 0.2 all-reduce.2.cloned.1.call-start
  55.0 213.0 %all-to-all-done.1 = bf16[32,2,256,512]{3,2,1,0:T(8,128)(2,1)} async-done(((bf16[32,2,256,512]{3,2,1,0:T(8,128)(2,1)}), bf16[32,2,256,512]{3,2,1,0:T(8,128)(2,1)}, u32[]{:S(2)}, u32[]{:S(2)}) %all-to-all-start.1) | async-done | bytes 16777248 | tf_op jit(solution)/shard_map/all_to_all | solution.py:35
  268.0 13.3 %gather_fusion.1 = bf16[62,256,512]{2,1,0:T(8,128)(2,1)} fusion(bf16[64,256,512]{2,1,0:T(8,128)(2,1)} %bitcast.6, s32[1024]{0:T(1024)S(1)} %pad_clamp_fusion.2), kind=kCustom, calls=%fused_computation.3 | custom fusion | bytes 32506104 | tf_op jit(solution)/shard_map/jit(_take)/gather | solution.py:42
  281.3 11.8 %fusion.7 = bf16[62,512,128]{2,1,0:T(8,128)(2,1)} fusion(bf16[62,256,128]{2,1,0:T(8,128)(2,1)} %bitcast.83, bf16[62,256,512]{2,1,0:T(8,128)(2,1)} %gather_fusion.1, pred[62]{0:T(512)(128)(4,1)S(1)} %compare_and_fusion), kind=kOutput, calls=%fused_computation.16 | convolution fusion | flops 2092564480 | bytes 28442686 | tf_op jit(solution)/shard_map/hdp,hdq->hpq/dot_general | solution.py:43
  293.1 6.0 fusion.11
  299.1 0.0 all-reduce.2.cloned.1.call-update
  299.1 0.0 copy-done.3
  299.2 0.7 gather_fusion.3
  299.9 0.7 gather_fusion.2
  300.6 0.1 iota_compare_fusion.1
  300.7 52.8 %all-reduce.2.cloned.1.call-done = f32[31,128,128]{2,1,0:T(8,128)} async-done(((f32[31,128,128]{2,1,0:T(8,128)}), f32[31,128,128]{2,1,0:T(8,128)}) %all-reduce.2.cloned.1.call-update) | async-done | bytes 2031632 | tf_op jit(solution)/shard_map/psum | solution.py:50
  353.5 2.3 copy.67
  355.8 2.7 broadcast_multiply_fusion
  358.5 2.9 copy.68
  361.4 4.0 fusion.13
  365.3 5.5 convert_bitcast_fusion.1
  370.8 3.2 convert_bitcast_fusion.2
  374.0 4.1 pad_maximum_fusion
  378.2 4.3 copy.71
  382.4 11.3 %convert_bitcast_fusion = bf16[62,256,512]{1,2,0:T(8,128)(2,1)} fusion(bf16[62,128,512]{2,1,0:T(8,128)(2,1)} %bitcast.82, bf16[62,256,128]{2,1,0:T(8,128)(2,1)} %bitcast.84), kind=kOutput, calls=%fused_computation.10 | convolution fusion | flops 2088501248 | bytes 28442624 | tf_op jit(solution)/shard_map/hdp,hpq->hdq/dot_general | solution.py:67
  393.7 21.9 %copy.73 = bf16[62,256,512]{2,1,0:T(8,128)(2,1)} copy(bf16[62,256,512]{1,2,0:T(8,128)(2,1)} %convert_bitcast_fusion) | data formatting | bytes 32505856 | tf_op jit(solution)/shard_map/convert_element_type | solution.py:69
  415.6 5.9 broadcast.266
  421.5 41.9 %scatter_fusion = bf16[64,256,512]{2,1,0:T(8,128)(2,1)} fusion(bf16[64,256,512]{2,1,0:T(8,128)(2,1)} %broadcast.266, s32[62]{0:T(128)S(1)} %fusion.22, bf16[62,256,512]{2,1,0:T(8,128)(2,1)} %copy.73), kind=kCustom, calls=%fused_computation.5 | custom fusion | bytes 48759032 | tf_op jit(solution)/shard_map/scatter | solution.py:70
  463.4 7.3 %all-to-all-start.2 = ((bf16[32,2,256,512]{3,2,1,0:T(8,128)(2,1)}), bf16[32,2,256,512]{3,2,1,0:T(8,128)(2,1)}, u32[]{:S(2)}, u32[]{:S(2)}) async-start(bf16[32,2,256,512]{3,2,1,0:T(8,128)(2,1)} %bitcast.80), calls=%async_computation.2 | async-start | bytes 33554432 | tf_op jit(solution)/shard_map/all_to_all | solution.py:71
  470.6 0.1 copy.69
  470.7 0.1 gt.19
  470.9 0.5 broadcast_multiply_fusion.1
  471.4 212.5 %all-to-all-done.2 = bf16[32,2,256,512]{3,2,1,0:T(8,128)(2,1)} async-done(((bf16[32,2,256,512]{3,2,1,0:T(8,128)(2,1)}), bf16[32,2,256,512]{3,2,1,0:T(8,128)(2,1)}, u32[]{:S(2)}, u32[]{:S(2)}) %all-to-all-start.2) | async-done | bytes 16777248 | tf_op jit(solution)/shard_map/all_to_all | solution.py:71
  683.9 16.8 %fusion = f32[16,256,512]{2,0,1:T(8,128)S(1)} fusion(s32[64]{0:T(128)S(1)} %reshape.269, pred[64]{0:T(512)(128)(4,1)S(1)} %gt.19, bf16[8,8,256,512]{3,2,1,0:T(8,128)(2,1)} %bitcast.32), kind=kOutput, calls=%fused_computation.6 | convolution fusion | flops 268437504 | bytes 25166144 | tf_op jit(solution)/shard_map/dot_general | solution.py:82
  700.6 8.3 %copy.75 = f32[16,256,512]{2,1,0:T(8,128)} copy(f32[16,256,512]{2,0,1:T(8,128)S(1)} %fusion) | data formatting | bytes 16777216
  (23 shorter events, 0.1 us)
Async XLA Ops:
  7.2 292.0 %copy-start = (f32[512]{0:T(512)S(1)}, f32[512]{0:T(512)}, u32[]{:S(2)}) copy-start(f32[512]{0:T(512)} %param.9) | copy-start | bytes 6148
  49.6 218.4 %all-to-all-start.1 = ((bf16[32,2,256,512]{3,2,1,0:T(8,128)(2,1)}), bf16[32,2,256,512]{3,2,1,0:T(8,128)(2,1)}, u32[]{:S(2)}, u32[]{:S(2)}) async-start(bf16[32,2,256,512]{3,2,1,0:T(8,128)(2,1)} %select_select_fusion), calls=%async_computation.1 | async-start | bytes 33554432 | tf_op jit(solution)/shard_map/all_to_all | solution.py:35
  54.8 298.7 %all-reduce.2.cloned.1.call-start = ((), (), s32[]{:S(2)}) async-start(), calls=%async_computation.3 | async-start | bytes 4063232 | tf_op jit(solution)/shard_map/psum | solution.py:50
  293.1 6.0 copy-start.3
  293.1 7.5 %copy-start.4 = (s32[31]{0:T(128)S(1)}, s32[31]{0:T(128)}, u32[]{:S(2)}) copy-start(s32[31]{0:T(128)} %param.11) | copy-start | bytes 376
  293.1 62.7 %copy-start.2 = (f32[31,128]{1,0:T(8,128)S(1)}, f32[31,128]{1,0:T(8,128)}, u32[]{:S(2)}) copy-start(f32[31,128]{1,0:T(8,128)} %param.12) | copy-start | bytes 47620
  361.4 9.5 %slice-start = ((s8[8126464]{0:T(1024)(128)(4,1)}), s8[4194304]{0:T(1024)(128)(4,1)S(1)}, s32[]{:S(2)}) async-start(s8[8126464]{0:T(1024)(128)(4,1)} %bitcast.87), calls=%async_computation.4 | async-start | bytes 8388608
  365.3 5.5 slice-start.1
  463.4 220.5 %all-to-all-start.2 = ((bf16[32,2,256,512]{3,2,1,0:T(8,128)(2,1)}), bf16[32,2,256,512]{3,2,1,0:T(8,128)(2,1)}, u32[]{:S(2)}, u32[]{:S(2)}) async-start(bf16[32,2,256,512]{3,2,1,0:T(8,128)(2,1)} %bitcast.80), calls=%async_computation.2 | async-start | bytes 33554432 | tf_op jit(solution)/shard_map/all_to_all | solution.py:71
  683.8 25.0 %copy-start.1 = (f32[512]{0:T(512)S(1)}, f32[512]{0:T(512)}, u32[]{:S(2)}) copy-start(f32[512]{0:T(512)} %param.9) | copy-start | bytes 6148
Sparse Core Ops, SparseCore 0:
  299.2 54.1 all-reduce.1
where the time goes:
time: 717 us; the launch traced here: 716 us
  waiting for transfers between devices  478 us (67%)
  local copies, waits for them, and re-layouts  114 us (16%)
  matrix products  54.5 us (8%)
  other arithmetic  26.1 us (4%)
  blocking collectives  15.6 us (2%)
  between operations  14.2 us (2%)
  starting transfers between devices  12.6 us (2%)
    all_to_all x1, waiting for transfers between devices, local(): lax.all_to_all(selected.reshape(groups, capacity, width_dom, width_aux),...  213 us
    all_to_all x1, waiting for transfers between devices, local(): lax.all_to_all(term_send.reshape(groups, capacity, width_dom, width_aux),...  212 us
    psum x1, waiting for transfers between devices, local(): coupling = lax.psum(partial_sum, 'aux')  52.8 us
    scatter x1, local copies, waits for them, and re-layouts, local(): jnp.zeros((slots, width_dom, width_aux), jnp.bfloat16).at[slot_of]  41.9 us
    convert_element_type x1, local copies, waits for them, and re-layouts, local(): dom_terms = jnp.einsum('hdp,hpq->hdq', coef_half, gamma, preferred_elemen...  21.9 us
    dot_general x1, matrix products, local(): jnp.dot(occ_hot.astype(jnp.bfloat16), terms.reshape(slots, width_dom * wi...  16.8 us
    all_to_all x1, blocking collectives, local(): lax.all_to_all(request.reshape(groups, capacity), 'pair', split_axis=0, c...  15.6 us
  transfers between devices with their start and end apart: 3, of which 3 were waited for; matrix products, arithmetic and copies ran while one was open for 0% of the time, Pallas kernels for 0%

commit v1 on v0

--- a/solution.py
+++ b/solution.py
@@ -5,6 +5,17 @@
 
 
 def local(three_index, fock_diag, pair_occ, pno_count, pno_energy, pno_coef):
+
+    def _mark_sheets(mesh_ax, z_in):
+        axis_n = lax.axis_size(mesh_ax)
+        u1 = z_in
+        q_next = lambda block_now: [(jj, jj ^ block_now) for jj in range(axis_n)]
+        for t in range(axis_n.bit_length() - 1):
+            work_now = q_next(1 << t)
+            extra = lax.ppermute(u1, axis_name=mesh_ax, perm=work_now)
+            u1 = u1 + extra
+        return u1
+
     groups = lax.axis_size("pair")
     occ_dev = three_index.shape[0]
     width_dom = three_index.shape[1]
@@ -47,7 +58,7 @@
     rows_i = paired[:, 0]
     rows_j = paired[:, 1]
     partial_sum = jnp.einsum("kpq,krq->kpr", rows_i, rows_j, preferred_element_type=jnp.float32)
-    coupling = lax.psum(partial_sum, "aux")
+    coupling = _mark_sheets("aux", partial_sum)
     fock_i = jnp.take(fock_diag, pair_occ[:, 0])
     fock_j = jnp.take(fock_diag, pair_occ[:, 1])
     denom = pno_energy[:, :, None] + pno_energy[:, None, :] - (fock_i + fock_j)[:, None, None]

time: 717 us -> 740 us (1.032)
  waiting for transfers between devices: 478 us -> 498 us
  between operations: 14.2 us -> 0.81 us
  starting transfers between devices: 12.6 us -> 25.5 us
    ppermute x0 -> x2, waiting for transfers between devices: none -> 72.7 us  [_mark_sheets(): extra = lax.ppermute(u1, axis_name=mesh_ax, perm=work_now)]
    psum x1 -> x0, waiting for transfers between devices: 52.8 us -> none  [local(): coupling = lax.psum(partial_sum, 'aux')]
  transfers between devices with their start and end apart: 3 -> 4, of which waited for: 3 -> 4; matrix products, arithmetic and copies ran while one was open for 0% -> 0% of each run, Pallas kernels for 0% -> 0%
where the time goes in v1:
time: 740 us; the launch traced here: 738 us
  waiting for transfers between devices  498 us (67%)
  local copies, waits for them, and re-layouts  114 us (15%)
  matrix products  53.2 us (7%)
  other arithmetic  30.6 us (4%)
  starting transfers between devices  25.5 us (3%)
  blocking collectives  15.6 us (2%)
    all_to_all x1, waiting for transfers between devices, local(): lax.all_to_all(selected.reshape(groups, capacity, width_dom, width_aux),...  213 us
    all_to_all x1, waiting for transfers between devices, local(): lax.all_to_all(term_send.reshape(groups, capacity, width_dom, width_aux),...  212 us
    ppermute x2, waiting for transfers between devices, _mark_sheets(): extra = lax.ppermute(u1, axis_name=mesh_ax, perm=work_now)  72.7 us
    scatter x1, local copies, waits for them, and re-layouts, local(): jnp.zeros((slots, width_dom, width_aux), jnp.bfloat16).at[slot_of]  42 us
    convert_element_type x1, local copies, waits for them, and re-layouts, local(): dom_terms = jnp.einsum('hdp,hpq->hdq', coef_half, gamma, preferred_elemen...  21.9 us
    dot_general x1, matrix products, local(): jnp.dot(occ_hot.astype(jnp.bfloat16), terms.reshape(slots, width_dom * wi...  16.8 us
    all_to_all x1, blocking collectives, local(): lax.all_to_all(request.reshape(groups, capacity), 'pair', split_axis=0, c...  15.6 us
  transfers between devices with their start and end apart: 4, of which 4 were waited for; matrix products, arithmetic and copies ran while one was open for 0% of the time, Pallas kernels for 0%

profile of v1, /device:TPU:0, one launch (start us, length us, event | category | flops | bytes accessed | tf_op | source)
XLA Modules:
  0.0 738.1 jit_solution(15178846758751673193)
XLA Ops:
  0.6 0.8 copy.56
  1.4 0.1 reshape.245
  1.5 0.1 reshape.244
  1.7 0.1 reduce_window_sum.11
  1.8 0.2 select_reduce_fusion
  2.0 0.8 scatter_custom_fusion
  2.8 0.1 all_to_all.12
  2.9 15.6 %all_to_all.19 = s32[32,1,2]{2,1,0:T(1,128)S(1)} all-to-all(s32[32,1,2]{2,1,0:T(1,128)S(1)} %bitcast.90), channel_id=1, replica_groups=mesh['aux'=4,'pair'=32] {'pair'}, dimensions={0} | all-to-all | bytes 512 | tf_op jit(solution)/shard_map/all_to_all | solution.py:38
  18.5 0.1 copy.59
  18.6 0.1 copy.62
  18.7 0.1 copy.60
  18.8 0.1 copy.63
  18.9 0.1 reshape.269
  19.0 9.8 %gather_fusion = bf16[64,256,512]{2,1,0:T(8,128)(2,1)} fusion(bf16[16,256,512]{2,1,0:T(8,128)(2,1)} %param.8, s32[1024]{0:T(1024)S(1)} %pad_clamp_fusion.3), kind=kCustom, calls=%fused_computation.2 | custom fusion | bytes 33554688 | tf_op jit(solution)/shard_map/jit(_take)/gather | solution.py:43
  28.8 14.4 %select_select_fusion = bf16[32,2,256,512]{3,2,1,0:T(8,128)(2,1)} fusion(bf16[32,2,256,512]{3,2,1,0:T(8,128)(2,1)} %bitcast.81, pred[32,2]{1,0:T(8,128)(4,1)S(1)} %copy.62, pred[32,2]{1,0:T(8,128)(4,1)S(1)} %copy.60), kind=kLoop, calls=%fused_computation.9 | loop fusion | flops 16777216 | bytes 33554560 | tf_op jit(solution)/shard_map/jit(_where)/select_n | solution.py:44
  43.2 5.2 all-to-all-start.1
  48.4 213.2 %all-to-all-done.1 = bf16[32,2,256,512]{3,2,1,0:T(8,128)(2,1)} async-done(((bf16[32,2,256,512]{3,2,1,0:T(8,128)(2,1)}), bf16[32,2,256,512]{3,2,1,0:T(8,128)(2,1)}, u32[]{:S(2)}, u32[]{:S(2)}) %all-to-all-start.1) | async-done | bytes 16777248 | tf_op jit(solution)/shard_map/all_to_all | solution.py:46
  261.6 13.3 %gather_fusion.1 = bf16[62,256,512]{2,1,0:T(8,128)(2,1)} fusion(bf16[64,256,512]{2,1,0:T(8,128)(2,1)} %bitcast.6, s32[1024]{0:T(1024)S(1)} %pad_clamp_fusion.2), kind=kCustom, calls=%fused_computation.3 | custom fusion | bytes 32506104 | tf_op jit(solution)/shard_map/jit(_take)/gather | solution.py:53
  274.8 11.8 %fusion.7 = bf16[62,512,128]{2,1,0:T(8,128)(2,1)} fusion(bf16[62,256,128]{2,1,0:T(8,128)(2,1)} %bitcast.83, bf16[62,256,512]{2,1,0:T(8,128)(2,1)} %gather_fusion.1, pred[62]{0:T(512)(128)(4,1)S(1)} %compare_and_fusion), kind=kOutput, calls=%fused_computation.16 | convolution fusion | flops 2092564480 | bytes 28442686 | tf_op jit(solution)/shard_map/hdp,hdq->hpq/dot_general | solution.py:54
  286.7 4.7 fusion.11
  291.4 1.6 collective-permute-start
  292.9 40.7 %collective-permute-done = f32[31,128,128]{2,1,0:T(8,128)S(1)} collective-permute-done((f32[31,128,128]{2,1,0:T(8,128)S(1)}, f32[31,128,128]{2,1,0:T(8,128)S(1)}, u32[]{:S(2)}, u32[]{:S(2)}) %collective-permute-start) | collective-permute-done | bytes 2031648 | tf_op jit(solution)/shard_map/ppermute | solution.py:15
  333.7 0.3 add.115
  334.0 4.3 collective-permute-start.1
  338.3 0.7 gather_fusion.3
  339.0 0.7 gather_fusion.2
  339.7 0.1 iota_compare_fusion.1
  339.8 32.0 %collective-permute-done.1 = f32[31,128,128]{2,1,0:T(8,128)} collective-permute-done((f32[31,128,128]{2,1,0:T(8,128)S(1)}, f32[31,128,128]{2,1,0:T(8,128)}, u32[]{:S(2)}, u32[]{:S(2)}) %collective-permute-start.1) | collective-permute-done | bytes 2031648 | tf_op jit(solution)/shard_map/ppermute | solution.py:15
  371.8 2.4 add.116
  374.2 2.1 copy.67
  376.3 4.4 broadcast_multiply_fusion
  380.7 2.9 copy.68
  383.6 4.0 fusion.13
  387.6 5.5 convert_bitcast_fusion.1
  393.0 3.2 convert_bitcast_fusion.2
  396.2 4.1 pad_maximum_fusion
  400.4 4.3 copy.71
  404.6 11.3 %convert_bitcast_fusion = bf16[62,256,512]{1,2,0:T(8,128)(2,1)} fusion(bf16[62,128,512]{2,1,0:T(8,128)(2,1)} %bitcast.82, bf16[62,256,128]{2,1,0:T(8,128)(2,1)} %bitcast.84), kind=kOutput, calls=%fused_computation.10 | convolution fusion | flops 2088501248 | bytes 28442624 | tf_op jit(solution)/shard_map/hdp,hpq->hdq/dot_general | solution.py:78
  415.9 21.9 %copy.73 = bf16[62,256,512]{2,1,0:T(8,128)(2,1)} copy(bf16[62,256,512]{1,2,0:T(8,128)(2,1)} %convert_bitcast_fusion) | data formatting | bytes 32505856 | tf_op jit(solution)/shard_map/convert_element_type | solution.py:80
  437.8 5.9 broadcast.266
  443.7 42.0 %scatter_fusion = bf16[64,256,512]{2,1,0:T(8,128)(2,1)} fusion(bf16[64,256,512]{2,1,0:T(8,128)(2,1)} %broadcast.266, s32[62]{0:T(128)S(1)} %fusion.22, bf16[62,256,512]{2,1,0:T(8,128)(2,1)} %copy.73), kind=kCustom, calls=%fused_computation.5 | custom fusion | bytes 48759032 | tf_op jit(solution)/shard_map/scatter | solution.py:81
  485.6 14.4 %all-to-all-start.2 = ((bf16[32,2,256,512]{3,2,1,0:T(8,128)(2,1)}), bf16[32,2,256,512]{3,2,1,0:T(8,128)(2,1)}, u32[]{:S(2)}, u32[]{:S(2)}) async-start(bf16[32,2,256,512]{3,2,1,0:T(8,128)(2,1)} %bitcast.80), calls=%async_computation.2 | async-start | bytes 33554432 | tf_op jit(solution)/shard_map/all_to_all | solution.py:82
  500.1 0.1 copy.69
  500.2 0.1 gt.19
  500.3 0.5 broadcast_multiply_fusion.1
  500.8 212.3 %all-to-all-done.2 = bf16[32,2,256,512]{3,2,1,0:T(8,128)(2,1)} async-done(((bf16[32,2,256,512]{3,2,1,0:T(8,128)(2,1)}), bf16[32,2,256,512]{3,2,1,0:T(8,128)(2,1)}, u32[]{:S(2)}, u32[]{:S(2)}) %all-to-all-start.2) | async-done | bytes 16777248 | tf_op jit(solution)/shard_map/all_to_all | solution.py:82
  713.1 16.8 %fusion = f32[16,256,512]{2,0,1:T(8,128)S(1)} fusion(s32[64]{0:T(128)S(1)} %reshape.269, pred[64]{0:T(512)(128)(4,1)S(1)} %gt.19, bf16[8,8,256,512]{3,2,1,0:T(8,128)(2,1)} %bitcast.32), kind=kOutput, calls=%fused_computation.6 | convolution fusion | flops 268437504 | bytes 25166144 | tf_op jit(solution)/shard_map/dot_general | solution.py:93
  729.8 8.3 %copy.75 = f32[16,256,512]{2,1,0:T(8,128)} copy(f32[16,256,512]{2,0,1:T(8,128)S(1)} %fusion) | data formatting | bytes 16777216
  (28 shorter events, 0.2 us)
Async XLA Ops:
  0.6 337.7 %copy-start = (f32[512]{0:T(512)S(1)}, f32[512]{0:T(512)}, u32[]{:S(2)}) copy-start(f32[512]{0:T(512)} %param.9) | copy-start | bytes 6148
  43.2 218.4 %all-to-all-start.1 = ((bf16[32,2,256,512]{3,2,1,0:T(8,128)(2,1)}), bf16[32,2,256,512]{3,2,1,0:T(8,128)(2,1)}, u32[]{:S(2)}, u32[]{:S(2)}) async-start(bf16[32,2,256,512]{3,2,1,0:T(8,128)(2,1)} %select_select_fusion), calls=%async_computation.1 | async-start | bytes 33554432 | tf_op jit(solution)/shard_map/all_to_all | solution.py:46
  286.7 51.6 %copy-start.4 = (s32[31,2]{0,1:T(2,128)S(1)}, s32[31,2]{0,1:T(2,128)}, u32[]{:S(2)}) copy-start(s32[31,2]{0,1:T(2,128)} %param.10) | copy-start | bytes 748
  286.7 53.1 %copy-start.5 = (s32[31]{0:T(128)S(1)}, s32[31]{0:T(128)}, u32[]{:S(2)}) copy-start(s32[31]{0:T(128)} %param.11) | copy-start | bytes 376
  291.3 85.0 %copy-start.3 = (f32[31,128]{1,0:T(8,128)S(1)}, f32[31,128]{1,0:T(8,128)}, u32[]{:S(2)}) copy-start(f32[31,128]{1,0:T(8,128)} %param.12) | copy-start | bytes 47620
  291.4 42.3 %collective-permute-start = (f32[31,128,128]{2,1,0:T(8,128)S(1)}, f32[31,128,128]{2,1,0:T(8,128)S(1)}, u32[]{:S(2)}, u32[]{:S(2)}) collective-permute-start(f32[31,128,128]{2,1,0:T(8,128)S(1)} %fusion.11), channel_id=1, source_target_pairs={{0,32},{32,0},{64,96},{96,64},{1,33},{33,1},{65,97},{97,65},{2,34}... | collective-permute-start | bytes 6094856 | tf_op jit(solution)/shard_map/ppermute | solution.py:15
  334.0 5.9 copy-start.2
  334.0 37.8 %collective-permute-start.1 = (f32[31,128,128]{2,1,0:T(8,128)S(1)}, f32[31,128,128]{2,1,0:T(8,128)}, u32[]{:S(2)}, u32[]{:S(2)}) collective-permute-start(f32[31,128,128]{2,1,0:T(8,128)S(1)} %add.115), channel_id=1, source_target_pairs={{0,64},{32,96},{64,0},{96,32},{1,65},{33,97},{65,1},{97,33},{2,66}... | collective-permute-start | bytes 6094856 | tf_op jit(solution)/shard_map/ppermute | solution.py:15
  383.6 9.5 %slice-start = ((s8[8126464]{0:T(1024)(128)(4,1)}), s8[4194304]{0:T(1024)(128)(4,1)S(1)}, s32[]{:S(2)}) async-start(s8[8126464]{0:T(1024)(128)(4,1)} %bitcast.87), calls=%async_computation.3 | async-start | bytes 8388608
  387.5 5.5 slice-start.1
  485.6 227.4 %all-to-all-start.2 = ((bf16[32,2,256,512]{3,2,1,0:T(8,128)(2,1)}), bf16[32,2,256,512]{3,2,1,0:T(8,128)(2,1)}, u32[]{:S(2)}, u32[]{:S(2)}) async-start(bf16[32,2,256,512]{3,2,1,0:T(8,128)(2,1)} %bitcast.80), calls=%async_computation.2 | async-start | bytes 33554432 | tf_op jit(solution)/shard_map/all_to_all | solution.py:82
  713.1 25.0 %copy-start.1 = (f32[512]{0:T(512)S(1)}, f32[512]{0:T(512)}, u32[]{:S(2)}) copy-start(f32[512]{0:T(512)} %param.9) | copy-start | bytes 6148
